TPU v7x, 256 devices: a whole 4x4x8 slice. The times are simulated.
256 devices in a mesh: clip: 16 (over z_lo, x), seq: 16 (over y, z_hi, core).
Axes of the slice: x: 4, y: 4, z: 8 (z_hi: 2, z_lo: 4; z = z_hi * 4 + z_lo), core: 2. Of those that a mesh axis runs over, the one named last changes fastest.
Arguments:
- t_query: bfloat16 [16, 4096, 1408], P('clip', 'seq'), may hold values from -8 to 8
- t_key: bfloat16 [16, 4096, 1408], P('clip', 'seq'), may hold values from -8 to 8
- t_value: bfloat16 [16, 4096, 1408], P('clip', 'seq'), may hold values from -6 to 6
- context: bfloat16 [16, 4096, 384], P('clip', 'seq'), may hold values from -6 to 6
- mask_list: int32 [16, 16, 256], P('clip'), may hold values from -1 to 4095, as said below
- block_owner: int32 [16, 16], P('clip'), may hold values from 0 to 15, each once within a row
- p_gain: float32 [384], replicated, may hold values from 0.25 to 1.75
- w_query: bfloat16 [384, 384], replicated, may hold values from -0.3125 to 0.3125
- w_key: bfloat16 [384, 384], replicated, may hold values from -0.3125 to 0.3125
- w_value: bfloat16 [384, 384], replicated, may hold values from -0.3125 to 0.3125
- w_proj: bfloat16 [384, 1408], replicated, may hold values from -0.3125 to 0.3125
Outputs:
- prediction: bfloat16 [16, 4096, 1408], P('clip', 'seq')
- loss: float32 [16], P('clip')
- grad_proj: float32 [384, 1408], P('clip', 'seq')
Inputs may be any that keep to these rules, and one draw needn't show every extreme that they name: `mask_list`: in block b of a clip, slots s * 16 to (s + 1) * 16 - 1 hold distinct positions of tokens s * 256 to (s + 1) * 256 - 1, filled slots first, then -1; a position appears at most once in a clip; in every clip one block has all slots filled, and some block has an empty slot; the last token of a clip is masked in every clip.
All inputs are finite; a program needn't handle non-finite values.
Results may differ from a plain program's by a relative error of at most 0.014.
Values may be sent and summed in bfloat16 or wider, within the bound.
No kernel may reach another device: no remote copies, remote signals or barrier semaphores. Data moves between devices by JAX's collectives and lax.ppermute only.
A program may use at most 128 MiB of HBM per device.

v0:
```python
import math

import jax
import jax.numpy as jnp
from jax import lax
from jax.experimental import pallas as pl
from jax.experimental.pallas import tpu as pltpu
from jax.sharding import PartitionSpec as P

TARGET_WIDTH = 1408
TARGET_HEADS = 16
HEAD = TARGET_WIDTH // TARGET_HEADS
PRED_WIDTH = 384
PRED_HEADS = 12
PRED_HEAD = PRED_WIDTH // PRED_HEADS
BLOCK_ROWS = 256
TOK = 256
N_SEQ = 16
TOKENS = TOK * N_SEQ
SLOTS = BLOCK_ROWS // N_SEQ
WINDOW = 256
LANES = 128
PIECE = 3 * HEAD
SCALE = math.log2(math.e) / math.sqrt(HEAD)
PRED_SCALE = math.log2(math.e) / math.sqrt(PRED_HEAD)

BF16 = jnp.bfloat16
F32 = jnp.float32


def mm(a, b):
    return jnp.dot(a, b, preferred_element_type=F32)


def mm_nt(a, b):
    return lax.dot_general(a, b, (((1,), (1,)), ((), ())), preferred_element_type=F32)


def iota(shape, dim):
    return lax.broadcasted_iota(jnp.int32, shape, dim)


def one_hot(mask):
    return jnp.where(mask, 1.0, 0.0).astype(BF16)


def spread_row(values, source):
    pick = one_hot(iota((BLOCK_ROWS, BLOCK_ROWS), 0) == source * SLOTS + iota((BLOCK_ROWS, BLOCK_ROWS), 1) % SLOTS)
    wide = mm(values.astype(BF16), pick)
    own = iota((N_SEQ, BLOCK_ROWS), 1) // SLOTS == iota((N_SEQ, BLOCK_ROWS), 0)
    return jnp.sum(jnp.where(own, wide, 0.0), axis=0, keepdims=True)


def earlier():
    return one_hot(iota((BLOCK_ROWS, BLOCK_ROWS), 0) < iota((BLOCK_ROWS, BLOCK_ROWS), 1))


def head_columns(head):
    start = min(head * HEAD // LANES * LANES, TARGET_WIDTH - WINDOW)
    return start, head * HEAD - start


def sender(piece, position):
    step = (position // 4 + 4 - piece // 4) % 4
    return step * 4 + ((position % 4) ^ (piece % 4))


def pack_kernel(me, owner, lists_in, query_in, keys_in, values_in, lists_out, send, lists, query, keys, values, sems):
    loads = [
        pltpu.make_async_copy(source, place, sems.at[i])
        for i, (source, place) in enumerate(
            [(lists_in, lists), (keys_in, keys), (values_in, values), (query_in, query)]
        )
    ]
    for load in loads:
        load.start()
    position = me[0]
    loads[0].wait()
    for b in range(N_SEQ):
        lists_out[pl.ds(owner[0, b], 1), :] = lists[b : b + 1, :]
    ordered = lists_out[...]
    row = spread_row(jnp.where(ordered >= 0, ordered - position * TOK, -1).astype(F32), position)
    valid = jnp.broadcast_to(row >= 0, (8, BLOCK_ROWS))
    rank = mm(one_hot(valid), earlier())[0:1]
    rank = jnp.where(row >= 0, rank, -1.0)
    place = iota((BLOCK_ROWS, BLOCK_ROWS), 0).astype(F32)
    compact = mm_nt(one_hot(rank == place), one_hot(row == place)).astype(BF16)
    for load in loads[1:]:
        load.wait()
    packed_query = mm(compact, query[...]).astype(BF16)
    for head in range(TARGET_HEADS):
        start, offset = head_columns(head)
        select = one_hot(iota((HEAD, WINDOW), 1) == iota((HEAD, WINDOW), 0) + offset)
        parts = [
            mm_nt(select, keys[:, start : start + WINDOW]),
            mm_nt(select, values[:, start : start + WINDOW]),
            mm_nt(select, packed_query[:, start : start + WINDOW]),
        ]
        send[head] = jnp.concatenate(parts, axis=0).astype(BF16)


def pack(me, owner, lists, query, keys, values):
    smem = pl.BlockSpec(memory_space=pltpu.SMEM)
    vmem = pl.BlockSpec(memory_space=pltpu.VMEM)
    hbm = pl.BlockSpec(memory_space=pltpu.HBM)
    return pl.pallas_call(
        pack_kernel,
        out_shape=(
            jax.ShapeDtypeStruct((N_SEQ, BLOCK_ROWS), jnp.int32),
            jax.ShapeDtypeStruct((TARGET_HEADS, PIECE, TOK), BF16),
        ),
        in_specs=[smem, smem] + [hbm] * 4,
        out_specs=(vmem, vmem),
        scratch_shapes=[
            pltpu.VMEM((N_SEQ, BLOCK_ROWS), jnp.int32),
            pltpu.VMEM((TOK, TARGET_WIDTH), BF16),
            pltpu.VMEM((TOK, TARGET_WIDTH), BF16),
            pltpu.VMEM((TOK, TARGET_WIDTH), BF16),
            pltpu.SemaphoreType.DMA((4,)),
        ],
        compiler_params=pltpu.CompilerParams(vmem_limit_bytes=56 * 2**20),
        cost_estimate=pl.CostEstimate(flops=3 * 10**9, bytes_accessed=5 * 10**6, transcendentals=0),
    )(me, owner, lists, query, keys, values)


def rank_kernel(lists, rank_out, local_out):
    ordered = lists[...]
    rows = []
    for source in range(N_SEQ):
        local = jnp.where(ordered >= 0, ordered - source * TOK, -1).astype(F32)
        rows.append(spread_row(local, source))
    local = jnp.concatenate(rows, axis=0)
    rank_out[...] = jnp.where(local >= 0, mm(one_hot(local >= 0), earlier()), -1.0)
    local_out[...] = jnp.concatenate([local, jnp.zeros((LANES - N_SEQ, BLOCK_ROWS), F32)], axis=0).T


def ranks(lists):
    vmem = pl.BlockSpec(memory_space=pltpu.VMEM)
    return pl.pallas_call(
        rank_kernel,
        out_shape=(
            jax.ShapeDtypeStruct((N_SEQ, BLOCK_ROWS), F32),
            jax.ShapeDtypeStruct((BLOCK_ROWS, LANES), F32),
        ),
        in_specs=[vmem],
        out_specs=(vmem, vmem),
        compiler_params=pltpu.CompilerParams(vmem_limit_bytes=8 * 2**20),
        cost_estimate=pl.CostEstimate(flops=10**9, bytes_accessed=10**5, transcendentals=0),
    )(lists)


def arrange_kernel(me, local, context, beyond, rows_out):
    for over, source in enumerate((context, beyond)):
        own = iota((BLOCK_ROWS, LANES), 1) == (me[0] ^ (2 * over))
        column = jnp.sum(jnp.where(own, local[...], 0.0), axis=1, keepdims=True)
        gather = one_hot(column == iota((BLOCK_ROWS, TOK), 1).astype(F32))
        rows_out[over] = mm(gather, source[...]).astype(BF16)


def arrange(me, local, context, beyond):
    smem = pl.BlockSpec(memory_space=pltpu.SMEM)
    vmem = pl.BlockSpec(memory_space=pltpu.VMEM)
    return pl.pallas_call(
        arrange_kernel,
        out_shape=jax.ShapeDtypeStruct((2, BLOCK_ROWS, PRED_WIDTH), BF16),
        in_specs=[smem] + [vmem] * 3,
        out_specs=vmem,
        compiler_params=pltpu.CompilerParams(vmem_limit_bytes=8 * 2**20),
        cost_estimate=pl.CostEstimate(flops=2 * 10**8, bytes_accessed=10**6, transcendentals=0),
    )(me, local, context, beyond)


def predict_kernel(me, lists, *refs):
    pieces = refs[:8]
    gain, w_query, w_key, w_value, hidden_out, context = refs[8:]
    position = me[0]
    for index in range(8):
        for over in range(2):
            source = sender((index % 4) * 4 + over * 2 + index // 4, position)
            rows = pieces[index][over].reshape(N_SEQ, SLOTS, PRED_WIDTH)
            context[:, pl.ds(pl.multiple_of(source * SLOTS, SLOTS), SLOTS), :] = rows

    def block(index, _):
        own = 2 * index + position % 2
        stream = context[own].astype(F32)
        mean = jnp.mean(stream, axis=1, keepdims=True)
        centered = stream - mean
        spread = jnp.mean(centered * centered, axis=1, keepdims=True)
        normed = (centered * lax.rsqrt(spread + 1e-6) * gain[...]).astype(BF16)
        queries = mm(normed, w_query[...]).astype(BF16)
        keys = mm(normed, w_key[...]).astype(BF16)
        values = mm(normed, w_value[...]).astype(BF16)
        key_valid = lists[pl.ds(own, 1), :] >= 0
        ones = jnp.ones((BLOCK_ROWS, LANES), BF16)
        groups = []
        for group in range(PRED_WIDTH // LANES):
            columns = slice(group * LANES, (group + 1) * LANES)
            with_ones = jnp.concatenate([values[:, columns], ones], axis=1)
            total = jnp.zeros((BLOCK_ROWS, LANES), F32)
            sums = jnp.ones((BLOCK_ROWS, LANES), F32)
            for head in range(LANES // PRED_HEAD):
                inside = iota((BLOCK_ROWS, LANES), 1) // PRED_HEAD == head
                masked = jnp.where(inside, queries[:, columns], jnp.zeros((), BF16))
                scores = jnp.where(key_valid, mm_nt(masked, keys[:, columns]), -1e30)
                most = jnp.max(scores, axis=1, keepdims=True)
                weights = jnp.exp2((scores - most) * PRED_SCALE)
                mixed = mm(weights.astype(BF16), with_ones)
                total = jnp.where(inside, mixed[:, :LANES], total)
                sums = jnp.where(inside, mixed[:, LANES:], sums)
            groups.append(total / sums)
        hidden_out[index] = (stream + jnp.concatenate(groups, axis=1)).astype(BF16)
        return 0

    lax.fori_loop(0, N_SEQ // 2, block, 0)


def predict(me, lists, pieces, gain, w_query, w_key, w_value):
    smem = pl.BlockSpec(memory_space=pltpu.SMEM)
    vmem = pl.BlockSpec(memory_space=pltpu.VMEM)
    return pl.pallas_call(
        predict_kernel,
        out_shape=jax.ShapeDtypeStruct((N_SEQ // 2, BLOCK_ROWS, PRED_WIDTH), BF16),
        in_specs=[smem] + [vmem] * 13,
        out_specs=vmem,
        scratch_shapes=[pltpu.VMEM((N_SEQ, BLOCK_ROWS, PRED_WIDTH), BF16)],
        compiler_params=pltpu.CompilerParams(vmem_limit_bytes=16 * 2**20),
        cost_estimate=pl.CostEstimate(flops=13 * 10**9, bytes_accessed=8 * 10**6, transcendentals=10**7),
    )(me, lists, *pieces, gain, w_query, w_key, w_value)


def project_kernel(me, lists, hidden, w_proj, pred_out):
    key_valid = lists[pl.ds(me[0], 1), :] >= 0
    square = (BLOCK_ROWS, BLOCK_ROWS)
    diagonal = jnp.where(iota(square, 0) == iota(square, 1), jnp.where(key_valid, 1.0, 0.0), 0.0)
    row_valid = jnp.sum(diagonal, axis=1, keepdims=True) > 0.5
    pred_out[...] = jnp.where(row_valid, mm(hidden[me[0] // 2], w_proj[...]), 0.0).astype(BF16)


def project(me, lists, hidden, w_proj):
    smem = pl.BlockSpec(memory_space=pltpu.SMEM)
    vmem = pl.BlockSpec(memory_space=pltpu.VMEM)
    return pl.pallas_call(
        project_kernel,
        out_shape=jax.ShapeDtypeStruct((BLOCK_ROWS, TARGET_WIDTH), BF16),
        in_specs=[smem] + [vmem] * 3,
        out_specs=vmem,
        compiler_params=pltpu.CompilerParams(vmem_limit_bytes=8 * 2**20),
        cost_estimate=pl.CostEstimate(flops=3 * 10**8, bytes_accessed=10**6, transcendentals=0),
    )(me, lists, hidden, w_proj)


ROWS = 256
CHUNK = 1024
PACKED = TOKENS + TOK
LOW, HIGH = 2.0**-80, 2.0**100


def attend_tile(index, query_rows, key_t, value, result):
    rows = pl.ds(pl.multiple_of(index * ROWS, ROWS), ROWS)
    query = query_rows[rows, :]
    total = jnp.zeros((ROWS, LANES), F32)
    for chunk in range(TOKENS // CHUNK):
        span = slice(chunk * CHUNK, (chunk + 1) * CHUNK)
        weights = jnp.exp2(mm(query, key_t[:, span]) * SCALE).astype(BF16)
        total = total + mm(weights, value[span, :])
    sums = total[:, HEAD : HEAD + 1]
    result[rows, :] = (total / sums).astype(BF16)
    safe = (jnp.min(sums) > LOW) & (jnp.max(sums) < HIGH)

    @pl.when(jnp.logical_not(safe))
    def _():
        def peak(chunk, most):
            span = pl.ds(pl.multiple_of(chunk * TOK, TOK), TOK)
            return jnp.maximum(most, jnp.max(mm(query, key_t[:, span]), axis=1, keepdims=True))

        most = lax.fori_loop(0, TOKENS // TOK, peak, jnp.full((ROWS, 1), -1e30, F32))

        def mix(chunk, total):
            span = pl.ds(pl.multiple_of(chunk * TOK, TOK), TOK)
            weights = jnp.exp2((mm(query, key_t[:, span]) - most) * SCALE).astype(BF16)
            return total + mm(weights, value[span, :])

        total = lax.fori_loop(0, TOKENS // TOK, mix, jnp.zeros((ROWS, LANES), F32))
        result[rows, :] = (total / total[:, HEAD : HEAD + 1]).astype(BF16)


def attend_kernel(plan, rank, received, target_out, stats_out, key_t, value, packed, result, stats):
    packed[...] = jnp.zeros((PACKED, LANES), BF16)
    result[...] = jnp.zeros((PACKED, LANES), BF16)
    for source in range(N_SEQ):
        piece = received[source].astype(F32)
        rest = jnp.zeros((LANES - HEAD, TOK), F32)
        key_t[:, source * TOK : (source + 1) * TOK] = jnp.concatenate([piece[:HEAD], rest], axis=0).astype(BF16)
        with_ones = jnp.concatenate([piece[HEAD : 2 * HEAD], rest + 1.0], axis=0)
        value[source * TOK : (source + 1) * TOK, :] = with_ones.T.astype(BF16)
        queries = jnp.concatenate([piece[2 * HEAD :], rest], axis=0).T.astype(BF16)
        packed[pl.ds(pl.multiple_of(plan[source], SLOTS), TOK), :] = queries

    def tile(index, _):
        attend_tile(index, packed, key_t, value, result)
        return 0

    lax.fori_loop(0, plan[N_SEQ], tile, 0)
    place = iota((TOK, BLOCK_ROWS), 0).astype(F32)
    for source in range(N_SEQ):
        rows = result[pl.ds(pl.multiple_of(plan[source], SLOTS), TOK), :]
        unpack = one_hot(rank[source : source + 1, :] == place)
        target = lax.dot_general(rows, unpack, (((0,), (0,)), ((), ())), preferred_element_type=F32)[:HEAD]
        target_out[source] = target.astype(BF16)
        mean = jnp.mean(target, axis=0, keepdims=True)
        centered = target - mean
        stats[0, source : source + 1, :] = mean
        stats[1, source : source + 1, :] = jnp.sum(centered * centered, axis=0, keepdims=True)
    for other in range(TARGET_HEADS):
        stats_out[other] = stats[...]


def attend(plan, rank, received):
    smem = pl.BlockSpec(memory_space=pltpu.SMEM)
    vmem = pl.BlockSpec(memory_space=pltpu.VMEM)
    return pl.pallas_call(
        attend_kernel,
        out_shape=(
            jax.ShapeDtypeStruct((N_SEQ, HEAD, BLOCK_ROWS), BF16),
            jax.ShapeDtypeStruct((TARGET_HEADS, 2, N_SEQ, BLOCK_ROWS), F32),
        ),
        in_specs=[smem, vmem, vmem],
        out_specs=(vmem, vmem),
        scratch_shapes=[
            pltpu.VMEM((LANES, TOKENS), BF16),
            pltpu.VMEM((TOKENS, LANES), BF16),
            pltpu.VMEM((PACKED, LANES), BF16),
            pltpu.VMEM((PACKED, LANES), BF16),
            pltpu.VMEM((2, N_SEQ, BLOCK_ROWS), F32),
        ],
        compiler_params=pltpu.CompilerParams(vmem_limit_bytes=16 * 2**20),
        cost_estimate=pl.CostEstimate(flops=12 * 10**9, bytes_accessed=3 * 10**6, transcendentals=16 * 10**6),
    )(plan, rank, received)


def slot_rows(hidden, source):
    span = slice(source * SLOTS, (source + 1) * SLOTS)
    return hidden[:, span, :].reshape(BLOCK_ROWS, PRED_WIDTH)


def compare_kernel(me, count, rank, target, stats, mine, other, w_proj, slope_out, loss_out, hidden):
    position = me[0]
    for index in range(N_SEQ // 2):
        hidden[2 * index + position % 2] = mine[index]
        hidden[2 * index + 1 - position % 2] = other[index]
    first = position * HEAD
    start = jnp.minimum(first // LANES * LANES, TARGET_WIDTH - WINDOW)
    window = w_proj[:, pl.ds(pl.multiple_of(start, LANES), WINDOW)]
    select = one_hot(iota((HEAD, WINDOW), 1) == iota((HEAD, WINDOW), 0) + (first - start))
    proj = mm_nt(select, window).astype(BF16)
    means = stats[:, 0]
    mean = jnp.mean(means, axis=0)
    between = means - mean[None]
    spread = (jnp.sum(stats[:, 1], axis=0) + HEAD * jnp.sum(between * between, axis=0)) / TARGET_WIDTH
    scale = lax.rsqrt(spread + 1e-6)
    keep_all = rank[...] >= 0
    share = 1.0 / jnp.full((1, BLOCK_ROWS), count[0], F32)
    losses = jnp.zeros((HEAD, BLOCK_ROWS), F32)
    for source in range(N_SEQ):
        rows = slot_rows(hidden, source)
        pred = mm_nt(proj, rows)
        one = slice(source, source + 1)
        goal = (target[source].astype(F32) - mean[one]) * scale[one]
        diff = pred - goal
        keep = keep_all[one]
        size = jnp.abs(diff)
        huber = jnp.where(size < 1.0, 0.5 * diff * diff, size - 0.5)
        losses = losses + jnp.where(keep, huber, 0.0)
        slope = jnp.where(keep, jnp.clip(diff, -1.0, 1.0) * share, 0.0)
        slope_out[source] = slope.astype(BF16)
    loss_out[...] = jnp.broadcast_to(jnp.sum(losses), (8, LANES))


def compare(me, count, rank, target, stats, mine, other, w_proj):
    smem = pl.BlockSpec(memory_space=pltpu.SMEM)
    vmem = pl.BlockSpec(memory_space=pltpu.VMEM)
    return pl.pallas_call(
        compare_kernel,
        out_shape=(
            jax.ShapeDtypeStruct((N_SEQ, HEAD, BLOCK_ROWS), BF16),
            jax.ShapeDtypeStruct((8, LANES), F32),
            jax.ShapeDtypeStruct((N_SEQ, BLOCK_ROWS, PRED_WIDTH), BF16),
        ),
        in_specs=[smem, smem] + [vmem] * 6,
        out_specs=(vmem, vmem, vmem),
        compiler_params=pltpu.CompilerParams(vmem_limit_bytes=12 * 2**20),
        cost_estimate=pl.CostEstimate(flops=10**9, bytes_accessed=5 * 10**6, transcendentals=0),
    )(me, count, rank, target, stats, mine, other, w_proj)


def gradient_kernel(slope, hidden, grad_out):
    gradient = jnp.zeros((HEAD, PRED_WIDTH), F32)
    for source in range(N_SEQ):
        rows = slot_rows(hidden, source)
        gradient = gradient + mm(slope[source], rows)
    rest = jnp.zeros((LANES - HEAD, PRED_WIDTH), F32)
    grad_out[...] = jnp.concatenate([gradient, rest], axis=0).T


def project_gradient(slope, hidden):
    vmem = pl.BlockSpec(memory_space=pltpu.VMEM)
    return pl.pallas_call(
        gradient_kernel,
        out_shape=jax.ShapeDtypeStruct((PRED_WIDTH, LANES), F32),
        in_specs=[vmem] * 2,
        out_specs=vmem,
        compiler_params=pltpu.CompilerParams(vmem_limit_bytes=8 * 2**20),
        cost_estimate=pl.CostEstimate(flops=4 * 10**9, bytes_accessed=4 * 10**6, transcendentals=0),
    )(slope, hidden)


def exchange(pieces, axis):
    return lax.all_to_all(pieces, axis, split_axis=0, concat_axis=0, tiled=True)


def across(values, mask):
    return lax.ppermute(values, "seq", [(i, i ^ mask) for i in range(N_SEQ)])


def along(values, step):
    return lax.ppermute(values, "seq", [(i, (i + 4 * step) % N_SEQ) for i in range(N_SEQ)])


def body(
    t_query, t_key, t_value, context, mask_list, block_owner, p_gain, w_query, w_key, w_value, w_proj
):
    me = lax.axis_index("seq").astype(jnp.int32).reshape(1)
    beyond = across(context[0], 2)
    lists, send = pack(me, block_owner, mask_list[0], t_query[0], t_key[0], t_value[0])
    send, beyond = lax.optimization_barrier((send, beyond))
    received = exchange(send, "seq")
    rank, local = ranks(lists)
    pair = arrange(me, local, context[0], beyond)
    column = [pair] + [along(pair, step) for step in range(1, 4)]
    pieces = column + [across(part, 1) for part in column]
    filled = (mask_list[0] >= 0).astype(jnp.int32)
    per_source = jnp.sum(filled.reshape(N_SEQ, N_SEQ, SLOTS), axis=(0, 2))
    count = jnp.sum(per_source).astype(F32).reshape(1)
    padded = (per_source + SLOTS - 1) // SLOTS * SLOTS
    upper = jnp.arange(N_SEQ)[:, None] < jnp.arange(N_SEQ + 1)[None, :]
    starts = jnp.sum(jnp.where(upper, padded[:, None], 0), axis=0)
    last = jnp.arange(N_SEQ + 1) == N_SEQ
    plan = jnp.where(last, (starts + ROWS - 1) // ROWS, starts).astype(jnp.int32)
    hidden = predict(me, lists, pieces, p_gain.reshape(1, PRED_WIDTH), w_query, w_key, w_value)
    received, hidden = lax.optimization_barrier((received, hidden))
    others = across(hidden, 1)
    target, stats = attend(plan, rank, received)
    stats = exchange(stats, "seq")
    pred_out = project(me, lists, hidden, w_proj)
    slope, loss, rows = compare(me, count, rank, target, stats, hidden, others, w_proj)
    loss, slope = lax.optimization_barrier((loss, slope))
    loss = loss + across(loss, 2)
    gradient = project_gradient(slope, rows)
    loss, gradient = lax.optimization_barrier((loss, gradient))
    shares = exchange(gradient.reshape(N_SEQ, PRED_WIDTH // N_SEQ, LANES), "clip")
    for mask in (1, 4, 8):
        loss = loss + across(loss, mask)
    loss = loss[0, :1] / (count * TARGET_WIDTH)
    gradient = jnp.sum(shares, axis=0)[:, :HEAD]
    return (pred_out[None], loss, gradient)


def solution(mesh):
    in_specs = (
        P("clip", "seq", None),
        P("clip", "seq", None),
        P("clip", "seq", None),
        P("clip", "seq", None),
        P("clip", None, None),
        P("clip", None),
        P(),
        P(),
        P(),
        P(),
        P(),
    )
    out_specs = (P("clip", "seq", None), P("clip"), P("clip", "seq"))
    return jax.shard_map(body, mesh=mesh, in_specs=in_specs, out_specs=out_specs, check_vma=False)
```

profile of v0, /device:TPU:2, one launch (start us, length us, event | category | flops | bytes accessed | tf_op | source)
XLA Modules:
  0.0 221.4 jit_solution(17386971896912150331)
XLA Ops:
  0.6 7.3 %collective-permute-start = (bf16[256,384]{1,0:T(8,128)(2,1)}, bf16[256,384]{1,0:T(8,128)(2,1)S(1)}, u32[]{:S(2)}, u32[]{:S(2)}) collective-permute-start(bf16[256,384]{1,0:T(8,128)(2,1)} %bitcast.11), channel_id=1, source_target_pairs={{0,2},{1,3},{2,0},{3,1},{4,6},{5,7},{6,4},{7,5},{8,10},{9,11},{10,... | collective-permute-start | bytes 589832 | tf_op jit(solution)/shard_map/ppermute | solution.py:422
  7.9 5.9 %shard_map.130 = (s32[16,256]{1,0:T(8,128)}, bf16[16,264,256]{2,1,0:T(8,128)(2,1)}) custom-call(s32[1]{0:T(128)} %bitcast.me, s32[1,16]{1,0:T(1,128)} %owner.1, s32[16,256]{1,0:T(8,128)} %bitcast.14, bf16[256,1408]{1,0:T(8,128)(2,1)} %bitcast.16, bf16[256,1408]{1,0:T(8,128)(2,1)} %bitcast.17, bf16[256,1408]{1,0:T(8,128)(2,1)} %bitcast.18), custom_call_target="tpu_custom_call" | custom-call | flops 3000000000 | bytes 5000000 | tf_op jit(solution)/shard_map/pallas_call | solution.py:106
  13.8 0.0 copy-start.5
  13.8 12.6 %all-to-all-start = ((bf16[16,264,256]{2,1,0:T(8,128)(2,1)}), bf16[16,264,256]{2,1,0:T(8,128)(2,1)}, u32[]{:S(2)}, u32[]{:S(2)}) async-start(bf16[16,264,256]{2,1,0:T(8,128)(2,1)} %get-tuple-element.22), calls=%async_computation | async-start | bytes 4325376 | tf_op jit(solution)/shard_map/all_to_all | solution.py:418
  26.4 0.0 copy-start.4
  26.4 0.0 copy-start.9
  26.4 0.0 copy-start.10
  26.4 0.0 copy-start.6
  26.4 0.4 shard_map.131
  26.9 0.5 copy-done.4
  27.3 0.4 shard_map.132.refs_0_
  27.7 2.0 collective-permute-start.1
  29.6 2.7 %collective-permute-start.2 = (bf16[2,256,384]{2,1,0:T(8,128)(2,1)S(1)}, bf16[2,256,384]{2,1,0:T(8,128)(2,1)S(1)}, u32[]{:S(2)}, u32[]{:S(2)}) collective-permute-start(bf16[2,256,384]{2,1,0:T(8,128)(2,1)S(1)} %shard_map.132.refs_0_), channel_id=1, source_target_pairs={{0,8},{1,9},{2,10},{3,11},{4,12},{5,13},{6,14},{7,15},{8,0},{9,1},... | collective-permute-start | bytes 1179656 | tf_op jit(solution)/shard_map/ppermute | solution.py:426
  32.3 1.5 collective-permute-start.3
  33.8 0.6 convert_reduce_fusion
  34.4 0.1 reduce_sum.45
  34.5 0.1 reduce_sum.46
  34.6 0.1 collective-permute-start.4
  34.7 27.7 %collective-permute-done.1.refs_1_ = bf16[2,256,384]{2,1,0:T(8,128)(2,1)S(1)} collective-permute-done((bf16[2,256,384]{2,1,0:T(8,128)(2,1)S(1)}, bf16[2,256,384]{2,1,0:T(8,128)(2,1)S(1)}, u32[]{:S(2)}, u32[]{:S(2)}) %collective-permute-start.1) | collective-permute-done | bytes 393248 | tf_op jit(solution)/shard_map/ppermute | solution.py:426
  62.4 8.7 %collective-permute-done.2.refs_2_ = bf16[2,256,384]{2,1,0:T(8,128)(2,1)S(1)} collective-permute-done((bf16[2,256,384]{2,1,0:T(8,128)(2,1)S(1)}, bf16[2,256,384]{2,1,0:T(8,128)(2,1)S(1)}, u32[]{:S(2)}, u32[]{:S(2)}) %collective-permute-start.2) | collective-permute-done | bytes 393248 | tf_op jit(solution)/shard_map/ppermute | solution.py:426
  71.1 0.0 collective-permute-start.6
  71.1 0.5 collective-permute-start.7
  71.6 0.1 select_reduce_fusion
  71.8 1.1 collective-permute-done.6.refs_6_
  72.8 0.6 collective-permute-done.7.refs_7_
  73.4 1.0 copy-done.7
  74.3 1.0 copy-done.8
  75.3 14.3 %shard_map.133.hidden.mine = bf16[8,256,384]{2,1,0:T(8,128)(2,1)S(1)} custom-call(s32[1]{0:T(128)} %bitcast.me, s32[16,256]{1,0:T(8,128)S(1)} %copy-done.5, bf16[2,256,384]{2,1,0:T(8,128)(2,1)S(1)} %shard_map.132.refs_0_, bf16[2,256,384]{2,1,0:T(8,128)(2,1)S(1)} %collective-permute-done.1.refs_1_, bf16[2,256,384]{2,1,0:T(8,128)(2,1)S(1)} %collective-permute-done.2.refs_2_, ...), custom_call_target="tpu_custom_call" | custom-call | flops 12999999488 | bytes 8000000 | tf_op jit(solution)/shard_map/pallas_call | solution.py:220
  89.6 0.2 collective-permute-start.8
  89.8 73.0 %shard_map.135 = (bf16[16,88,256]{2,1,0:T(8,128)(2,1)S(1)}, f32[16,2,16,256]{3,2,1,0:T(8,128)S(1)}) custom-call(s32[17]{0:T(128)S(1)} %compare_select_fusion.plan, f32[16,256]{1,0:T(8,128)S(1)} %get-tuple-element.26.rank, bf16[16,264,256]{2,1,0:T(8,128)(2,1)} %all-to-all-done.received), custom_call_target="tpu_custom_call" | custom-call | flops 12000000000 | bytes 3000000 | tf_op jit(solution)/shard_map/pallas_call | solution.py:321
  162.8 0.0 copy-start.1
  162.8 0.8 copy-done.1
  163.6 0.8 copy-done.3
  164.4 6.9 %all-to-all-start.1 = ((f32[16,2,16,256]{3,2,1,0:T(8,128)}), f32[16,2,16,256]{3,2,1,0:T(8,128)S(1)}, u32[]{:S(2)}, u32[]{:S(2)}) async-start(f32[16,2,16,256]{3,2,1,0:T(8,128)} %copy-done.3), calls=%async_computation.1 | async-start | bytes 1048576 | tf_op jit(solution)/shard_map/all_to_all | solution.py:418
  171.9 14.1 %all-to-all-done.1.stats = f32[16,2,16,256]{3,2,1,0:T(8,128)S(1)} async-done(((f32[16,2,16,256]{3,2,1,0:T(8,128)}), f32[16,2,16,256]{3,2,1,0:T(8,128)S(1)}, u32[]{:S(2)}, u32[]{:S(2)}) %all-to-all-start.1) | async-done | bytes 524320 | tf_op jit(solution)/shard_map/all_to_all | solution.py:418
  186.1 1.1 copy-done.2
  187.2 3.3 %shard_map.136 = (bf16[16,88,256]{2,1,0:T(8,128)(2,1)S(1)}, f32[8,128]{1,0:T(8,128)S(1)}, bf16[16,256,384]{2,1,0:T(8,128)(2,1)S(1)}) custom-call(s32[1]{0:T(128)} %bitcast.me, f32[1]{0:T(128)} %bitcast.7.count, f32[16,256]{1,0:T(8,128)S(1)} %get-tuple-element.26.rank, bf16[16,88,256]{2,1,0:T(8,128)(2,1)S(1)} %copy-done.2, ...), custom_call_target="tpu_custom_call" | custom-call | flops 1000000000 | bytes 5000000 | tf_op jit(solution)/shard_map/pallas_call | solution.py:382
  190.5 0.9 collective-permute-start.9
  191.4 1.4 shard_map.137
  192.8 5.3 %collective-permute-done.9 = f32[8,128]{1,0:T(8,128)S(1)} collective-permute-done((f32[8,128]{1,0:T(8,128)S(1)}, f32[8,128]{1,0:T(8,128)S(1)}, u32[]{:S(2)}, u32[]{:S(2)}) %collective-permute-start.9) | collective-permute-done | bytes 4128 | tf_op jit(solution)/shard_map/ppermute | solution.py:422
  198.1 10.5 %all-to-all-start.2 = ((f32[16,24,128]{2,1,0:T(8,128)}), f32[16,24,128]{2,1,0:T(8,128)S(1)}, u32[]{:S(2)}, u32[]{:S(2)}) async-start(f32[16,24,128]{2,1,0:T(8,128)} %bitcast.9), calls=%async_computation.2 | async-start | bytes 393216 | tf_op jit(solution)/shard_map/all_to_all | solution.py:418
  208.6 1.2 collective-permute-done.10
  209.8 3.6 %collective-permute-done.11 = f32[8,128]{1,0:T(8,128)S(1)} collective-permute-done((f32[8,128]{1,0:T(8,128)S(1)}, f32[8,128]{1,0:T(8,128)S(1)}, u32[]{:S(2)}, u32[]{:S(2)}) %collective-permute-start.11) | collective-permute-done | bytes 4128 | tf_op jit(solution)/shard_map/ppermute | solution.py:422
  213.4 0.8 collective-permute-start.12
  214.2 1.4 shard_map.134
  215.6 2.9 %collective-permute-done.12 = f32[8,128]{1,0:T(8,128)S(1)} collective-permute-done((f32[8,128]{1,0:T(8,128)S(1)}, f32[8,128]{1,0:T(8,128)S(1)}, u32[]{:S(2)}, u32[]{:S(2)}) %collective-permute-start.12) | collective-permute-done | bytes 4128 | tf_op jit(solution)/shard_map/ppermute | solution.py:422
  218.5 0.5 slice.6
  219.7 0.6 reduce_sum.48
  (27 shorter events, 0.1 us)
Async XLA Ops:
  0.6 13.1 %collective-permute-start = (bf16[256,384]{1,0:T(8,128)(2,1)}, bf16[256,384]{1,0:T(8,128)(2,1)S(1)}, u32[]{:S(2)}, u32[]{:S(2)}) collective-permute-start(bf16[256,384]{1,0:T(8,128)(2,1)} %bitcast.11), channel_id=1, source_target_pairs={{0,2},{1,3},{2,0},{3,1},{4,6},{5,7},{6,4},{7,5},{8,10},{9,11},{10,... | collective-permute-start | bytes 589832 | tf_op jit(solution)/shard_map/ppermute | solution.py:422
  13.8 12.6 %copy-start.5 = (s32[16,256]{1,0:T(8,128)S(1)}, s32[16,256]{1,0:T(8,128)}, u32[]{:S(2)}) copy-start(s32[16,256]{1,0:T(8,128)} %get-tuple-element.20.lists) | copy-start | bytes 49156
  13.8 75.8 %all-to-all-start = ((bf16[16,264,256]{2,1,0:T(8,128)(2,1)}), bf16[16,264,256]{2,1,0:T(8,128)(2,1)}, u32[]{:S(2)}, u32[]{:S(2)}) async-start(bf16[16,264,256]{2,1,0:T(8,128)(2,1)} %get-tuple-element.22), calls=%async_computation | async-start | bytes 4325376 | tf_op jit(solution)/shard_map/all_to_all | solution.py:418
  26.4 0.9 copy-start.4
  26.4 7.4 %copy-start.9 = (s32[1,16,256]{2,1,0:T(8,128)S(1)}, s32[1,16,256]{2,1,0:T(8,128)}, u32[]{:S(2)}) copy-start(s32[1,16,256]{2,1,0:T(8,128)} %param.15) | copy-start | bytes 49156
  26.4 45.2 %copy-start.10 = (f32[384]{0:T(512)S(1)}, f32[384]{0:T(512)}, u32[]{:S(2)}) copy-start(f32[384]{0:T(512)} %param.17) | copy-start | bytes 4612
  26.4 46.9 %copy-start.6 = (bf16[384,384]{1,0:T(8,128)(2,1)S(1)}, bf16[384,384]{1,0:T(8,128)(2,1)}, u32[]{:S(2)}) copy-start(bf16[384,384]{1,0:T(8,128)(2,1)} %refs_9_.1) | copy-start | bytes 884740
  27.7 34.7 %collective-permute-start.1 = (bf16[2,256,384]{2,1,0:T(8,128)(2,1)S(1)}, bf16[2,256,384]{2,1,0:T(8,128)(2,1)S(1)}, u32[]{:S(2)}, u32[]{:S(2)}) collective-permute-start(bf16[2,256,384]{2,1,0:T(8,128)(2,1)S(1)} %shard_map.132.refs_0_), channel_id=1, source_target_pairs={{0,4},{1,5},{2,6},{3,7},{4,8},{5,9},{6,10},{7,11},{8,12},{9,13},{1... | collective-permute-start | bytes 1179656 | tf_op jit(solution)/shard_map/ppermute | solution.py:426
  29.6 41.5 %collective-permute-start.2 = (bf16[2,256,384]{2,1,0:T(8,128)(2,1)S(1)}, bf16[2,256,384]{2,1,0:T(8,128)(2,1)S(1)}, u32[]{:S(2)}, u32[]{:S(2)}) collective-permute-start(bf16[2,256,384]{2,1,0:T(8,128)(2,1)S(1)} %shard_map.132.refs_0_), channel_id=1, source_target_pairs={{0,8},{1,9},{2,10},{3,11},{4,12},{5,13},{6,14},{7,15},{8,0},{9,1},... | collective-permute-start | bytes 1179656 | tf_op jit(solution)/shard_map/ppermute | solution.py:426
  32.3 38.8 %collective-permute-start.3 = (bf16[2,256,384]{2,1,0:T(8,128)(2,1)S(1)}, bf16[2,256,384]{2,1,0:T(8,128)(2,1)S(1)}, u32[]{:S(2)}, u32[]{:S(2)}) collective-permute-start(bf16[2,256,384]{2,1,0:T(8,128)(2,1)S(1)} %shard_map.132.refs_0_), channel_id=1, source_target_pairs={{0,12},{1,13},{2,14},{3,15},{4,0},{5,1},{6,2},{7,3},{8,4},{9,5},{1... | collective-permute-start | bytes 1179656 | tf_op jit(solution)/shard_map/ppermute | solution.py:426
  34.6 37.1 %collective-permute-start.4 = (bf16[2,256,384]{2,1,0:T(8,128)(2,1)S(1)}, bf16[2,256,384]{2,1,0:T(8,128)(2,1)S(1)}, u32[]{:S(2)}, u32[]{:S(2)}) collective-permute-start(bf16[2,256,384]{2,1,0:T(8,128)(2,1)S(1)} %shard_map.132.refs_0_), channel_id=1, source_target_pairs={{0,1},{1,0},{2,3},{3,2},{4,5},{5,4},{6,7},{7,6},{8,9},{9,8},{10,11... | collective-permute-start | bytes 1179656 | tf_op jit(solution)/shard_map/ppermute | solution.py:422
  62.4 9.4 %collective-permute-start.5 = (bf16[2,256,384]{2,1,0:T(8,128)(2,1)S(1)}, bf16[2,256,384]{2,1,0:T(8,128)(2,1)S(1)}, u32[]{:S(2)}, u32[]{:S(2)}) collective-permute-start(bf16[2,256,384]{2,1,0:T(8,128)(2,1)S(1)} %collective-permute-done.1.refs_1_), channel_id=1, source_target_pairs={{0,1},{1,0},{2,3},{3,2},{4,5},{5,4},{6,7},{7,6},{8,9},{9,8},{10,11... | collective-permute-start | bytes 1179656 | tf_op jit(solution)/shard_map/ppermute | solution.py:422
  71.1 1.7 collective-permute-start.6
  71.1 2.3 %collective-permute-start.7 = (bf16[2,256,384]{2,1,0:T(8,128)(2,1)S(1)}, bf16[2,256,384]{2,1,0:T(8,128)(2,1)S(1)}, u32[]{:S(2)}, u32[]{:S(2)}) collective-permute-start(bf16[2,256,384]{2,1,0:T(8,128)(2,1)S(1)} %collective-permute-done.3.refs_3_), channel_id=1, source_target_pairs={{0,1},{1,0},{2,3},{3,2},{4,5},{5,4},{6,7},{7,6},{8,9},{9,8},{10,11... | collective-permute-start | bytes 1179656 | tf_op jit(solution)/shard_map/ppermute | solution.py:422
  73.4 1.0 copy-start.7
  74.3 1.0 copy-start.8
  89.6 96.5 %collective-permute-start.8 = (bf16[8,256,384]{2,1,0:T(8,128)(2,1)S(1)}, bf16[8,256,384]{2,1,0:T(8,128)(2,1)}, u32[]{:S(2)}, u32[]{:S(2)}) collective-permute-start(bf16[8,256,384]{2,1,0:T(8,128)(2,1)S(1)} %shard_map.133.hidden.mine), channel_id=1, source_target_pairs={{0,1},{1,0},{2,3},{3,2},{4,5},{5,4},{6,7},{7,6},{8,9},{9,8},{10,11... | collective-permute-start | bytes 4718600 | tf_op jit(solution)/shard_map/ppermute | solution.py:422
  89.8 96.3 %copy-start = (bf16[384,1408]{1,0:T(8,128)(2,1)S(1)}, bf16[384,1408]{1,0:T(8,128)(2,1)}, u32[]{:S(2)}) copy-start(bf16[384,1408]{1,0:T(8,128)(2,1)} %w_proj.3) | copy-start | bytes 3244036
  162.8 0.9 copy-start.1
  163.6 0.8 copy-start.3
  164.4 21.6 %all-to-all-start.1 = ((f32[16,2,16,256]{3,2,1,0:T(8,128)}), f32[16,2,16,256]{3,2,1,0:T(8,128)S(1)}, u32[]{:S(2)}, u32[]{:S(2)}) async-start(f32[16,2,16,256]{3,2,1,0:T(8,128)} %copy-done.3), calls=%async_computation.1 | async-start | bytes 1048576 | tf_op jit(solution)/shard_map/all_to_all | solution.py:418
  186.1 1.1 copy-start.2
  190.5 7.6 %collective-permute-start.9 = (f32[8,128]{1,0:T(8,128)S(1)}, f32[8,128]{1,0:T(8,128)S(1)}, u32[]{:S(2)}, u32[]{:S(2)}) collective-permute-start(f32[8,128]{1,0:T(8,128)S(1)} %get-tuple-element.32), channel_id=1, source_target_pairs={{0,2},{1,3},{2,0},{3,1},{4,6},{5,7},{6,4},{7,5},{8,10},{9,11},{10,... | collective-permute-start | bytes 12296 | tf_op jit(solution)/shard_map/ppermute | solution.py:422
  198.1 21.6 %all-to-all-start.2 = ((f32[16,24,128]{2,1,0:T(8,128)}), f32[16,24,128]{2,1,0:T(8,128)S(1)}, u32[]{:S(2)}, u32[]{:S(2)}) async-start(f32[16,24,128]{2,1,0:T(8,128)} %bitcast.9), calls=%async_computation.2 | async-start | bytes 393216 | tf_op jit(solution)/shard_map/all_to_all | solution.py:418
  208.6 1.2 collective-permute-start.10
  209.7 3.6 %collective-permute-start.11 = (f32[8,128]{1,0:T(8,128)S(1)}, f32[8,128]{1,0:T(8,128)S(1)}, u32[]{:S(2)}, u32[]{:S(2)}) collective-permute-start(f32[8,128]{1,0:T(8,128)S(1)} %add.32), channel_id=1, source_target_pairs={{0,4},{1,5},{2,6},{3,7},{4,0},{5,1},{6,2},{7,3},{8,12},{9,13},{10,... | collective-permute-start | bytes 12296 | tf_op jit(solution)/shard_map/ppermute | solution.py:422
  213.4 5.1 %collective-permute-start.12 = (f32[8,128]{1,0:T(8,128)S(1)}, f32[8,128]{1,0:T(8,128)S(1)}, u32[]{:S(2)}, u32[]{:S(2)}) collective-permute-start(f32[8,128]{1,0:T(8,128)S(1)} %add.33), channel_id=1, source_target_pairs={{0,8},{1,9},{2,10},{3,11},{4,12},{5,13},{6,14},{7,15},{8,0},{9,1},... | collective-permute-start | bytes 12296 | tf_op jit(solution)/shard_map/ppermute | solution.py:422
where the time goes:
time: 218 us; the launch traced here: 221 us
  Pallas kernels  100 us (46%)
  waiting for transfers between devices  65 us (30%)
  starting transfers between devices  45.9 us (21%)
  local copies, waits for them, and re-layouts  5.76 us (3%)
  between operations  3.27 us (2%)
    pallas_call x1, Pallas kernels, attend(): pl.pallas_call(attend_kernel, out_shape=(jax.ShapeDtypeStruct((N_SEQ, HEA...  73 us
    ppermute x3, waiting for transfers between devices, along(): lax.ppermute(values, 'seq', [(i, (i + 4 * step) % N_SEQ) for i in range(N...  36.4 us
    all_to_all x3, starting transfers between devices, exchange(): return lax.all_to_all(pieces, axis, split_axis=0, concat_axis=0, tiled=True)  29.9 us
    ppermute x10, waiting for transfers between devices, across(): return lax.ppermute(values, 'seq', [(i, i ^ mask) for i in range(N_SEQ)])  14.5 us
    pallas_call x1, Pallas kernels, predict(): pl.pallas_call(predict_kernel, out_shape=jax.ShapeDtypeStruct((N_SEQ // 2...  14.3 us
    all_to_all x3, waiting for transfers between devices, exchange(): return lax.all_to_all(pieces, axis, split_axis=0, concat_axis=0, tiled=True)  14.1 us
    ppermute x10, starting transfers between devices, across(): return lax.ppermute(values, 'seq', [(i, i ^ mask) for i in range(N_SEQ)])  9.81 us
    ppermute x3, starting transfers between devices, along(): lax.ppermute(values, 'seq', [(i, (i + 4 * step) % N_SEQ) for i in range(N...  6.09 us
  transfers between devices with their start and end apart: 16, of which 9 were waited for; matrix products, arithmetic and copies ran while one was open for 1% of the time, Pallas kernels for 44%

commit v1 on v0

--- a/solution.py
+++ b/solution.py
@@ -65,7 +65,7 @@
     return step * 4 + ((position % 4) ^ (piece % 4))
 
 
-def pack_kernel(me, owner, lists_in, query_in, keys_in, values_in, lists_out, send, lists, query, keys, values, sems):
+def pack_kernel(me, owner, lists_in, query_in, keys_in, values_in, send, lists, blocks, query, keys, values, sems):
     loads = [
         pltpu.make_async_copy(source, place, sems.at[i])
         for i, (source, place) in enumerate(
@@ -77,8 +77,8 @@
     position = me[0]
     loads[0].wait()
     for b in range(N_SEQ):
-        lists_out[pl.ds(owner[0, b], 1), :] = lists[b : b + 1, :]
-    ordered = lists_out[...]
+        blocks[pl.ds(owner[0, b], 1), :] = lists[b : b + 1, :]
+    ordered = blocks[...]
     row = spread_row(jnp.where(ordered >= 0, ordered - position * TOK, -1).astype(F32), position)
     valid = jnp.broadcast_to(row >= 0, (8, BLOCK_ROWS))
     rank = mm(one_hot(valid), earlier())[0:1]
@@ -105,13 +105,11 @@
     hbm = pl.BlockSpec(memory_space=pltpu.HBM)
     return pl.pallas_call(
         pack_kernel,
-        out_shape=(
-            jax.ShapeDtypeStruct((N_SEQ, BLOCK_ROWS), jnp.int32),
-            jax.ShapeDtypeStruct((TARGET_HEADS, PIECE, TOK), BF16),
-        ),
+        out_shape=jax.ShapeDtypeStruct((TARGET_HEADS, PIECE, TOK), BF16),
         in_specs=[smem, smem] + [hbm] * 4,
-        out_specs=(vmem, vmem),
+        out_specs=vmem,
         scratch_shapes=[
+            pltpu.VMEM((N_SEQ, BLOCK_ROWS), jnp.int32),
             pltpu.VMEM((N_SEQ, BLOCK_ROWS), jnp.int32),
             pltpu.VMEM((TOK, TARGET_WIDTH), BF16),
             pltpu.VMEM((TOK, TARGET_WIDTH), BF16),
@@ -123,8 +121,10 @@
     )(me, owner, lists, query, keys, values)
 
 
-def rank_kernel(lists, rank_out, local_out):
-    ordered = lists[...]
+def rank_kernel(owner, lists, lists_out, rank_out, local_out, plan_out, count_out):
+    for b in range(N_SEQ):
+        lists_out[pl.ds(owner[0, b], 1), :] = lists[b : b + 1, :]
+    ordered = lists_out[...]
     rows = []
     for source in range(N_SEQ):
         local = jnp.where(ordered >= 0, ordered - source * TOK, -1).astype(F32)
@@ -132,21 +132,34 @@
     local = jnp.concatenate(rows, axis=0)
     rank_out[...] = jnp.where(local >= 0, mm(one_hot(local >= 0), earlier()), -1.0)
     local_out[...] = jnp.concatenate([local, jnp.zeros((LANES - N_SEQ, BLOCK_ROWS), F32)], axis=0).T
-
-
-def ranks(lists):
+    start = jnp.int32(0)
+    count = jnp.int32(0)
+    for source in range(N_SEQ):
+        filled = jnp.sum(jnp.where(rows[source] >= 0, 1.0, 0.0)).astype(jnp.int32)
+        plan_out[source] = start
+        start = start + (filled + SLOTS - 1) // SLOTS * SLOTS
+        count = count + filled
+    plan_out[N_SEQ] = (start + ROWS - 1) // ROWS
+    count_out[0] = count.astype(F32)
+
+
+def ranks(owner, lists):
+    smem = pl.BlockSpec(memory_space=pltpu.SMEM)
     vmem = pl.BlockSpec(memory_space=pltpu.VMEM)
     return pl.pallas_call(
         rank_kernel,
         out_shape=(
+            jax.ShapeDtypeStruct((N_SEQ, BLOCK_ROWS), jnp.int32),
             jax.ShapeDtypeStruct((N_SEQ, BLOCK_ROWS), F32),
             jax.ShapeDtypeStruct((BLOCK_ROWS, LANES), F32),
+            jax.ShapeDtypeStruct((N_SEQ + 1,), jnp.int32),
+            jax.ShapeDtypeStruct((1,), F32),
         ),
-        in_specs=[vmem],
-        out_specs=(vmem, vmem),
+        in_specs=[smem, vmem],
+        out_specs=(vmem, vmem, vmem, smem, smem),
         compiler_params=pltpu.CompilerParams(vmem_limit_bytes=8 * 2**20),
         cost_estimate=pl.CostEstimate(flops=10**9, bytes_accessed=10**5, transcendentals=0),
-    )(lists)
+    )(owner, lists)
 
 
 def arrange_kernel(me, local, context, beyond, rows_out):
@@ -211,7 +224,7 @@
         hidden_out[index] = (stream + jnp.concatenate(groups, axis=1)).astype(BF16)
         return 0
 
-    lax.fori_loop(0, N_SEQ // 2, block, 0)
+    lax.fori_loop(0, N_SEQ // 2, block, 0, unroll=4)
 
 
 def predict(me, lists, pieces, gain, w_query, w_key, w_value):
@@ -228,80 +241,74 @@
     )(me, lists, *pieces, gain, w_query, w_key, w_value)
 
 
-def project_kernel(me, lists, hidden, w_proj, pred_out):
-    key_valid = lists[pl.ds(me[0], 1), :] >= 0
-    square = (BLOCK_ROWS, BLOCK_ROWS)
-    diagonal = jnp.where(iota(square, 0) == iota(square, 1), jnp.where(key_valid, 1.0, 0.0), 0.0)
-    row_valid = jnp.sum(diagonal, axis=1, keepdims=True) > 0.5
-    pred_out[...] = jnp.where(row_valid, mm(hidden[me[0] // 2], w_proj[...]), 0.0).astype(BF16)
-
-
-def project(me, lists, hidden, w_proj):
-    smem = pl.BlockSpec(memory_space=pltpu.SMEM)
-    vmem = pl.BlockSpec(memory_space=pltpu.VMEM)
-    return pl.pallas_call(
-        project_kernel,
-        out_shape=jax.ShapeDtypeStruct((BLOCK_ROWS, TARGET_WIDTH), BF16),
-        in_specs=[smem] + [vmem] * 3,
-        out_specs=vmem,
-        compiler_params=pltpu.CompilerParams(vmem_limit_bytes=8 * 2**20),
-        cost_estimate=pl.CostEstimate(flops=3 * 10**8, bytes_accessed=10**6, transcendentals=0),
-    )(me, lists, hidden, w_proj)
-
-
 ROWS = 256
+TILES = 3
 CHUNK = 1024
 PACKED = TOKENS + TOK
+MIXED = HEAD + 8
+STATS = 2 * N_SEQ
 LOW, HIGH = 2.0**-80, 2.0**100
 
 
-def attend_tile(index, query_rows, key_t, value, result):
-    rows = pl.ds(pl.multiple_of(index * ROWS, ROWS), ROWS)
-    query = query_rows[rows, :]
-    total = jnp.zeros((ROWS, LANES), F32)
+def attend_tile(first, extent, key, value_t, packed, result):
+    rows = pl.ds(pl.multiple_of(first * ROWS, ROWS), extent)
+    query_t = packed[rows, :].astype(F32).T.astype(BF16)
+    total = jnp.zeros((MIXED, extent), F32)
     for chunk in range(TOKENS // CHUNK):
         span = slice(chunk * CHUNK, (chunk + 1) * CHUNK)
-        weights = jnp.exp2(mm(query, key_t[:, span]) * SCALE).astype(BF16)
-        total = total + mm(weights, value[span, :])
-    sums = total[:, HEAD : HEAD + 1]
-    result[rows, :] = (total / sums).astype(BF16)
+        weights = jnp.exp2(mm(key[span, :], query_t) * SCALE).astype(BF16)
+        total = total + mm(value_t[:MIXED, span], weights)
+
+    def finish(total):
+        rest = jnp.zeros((LANES - MIXED, extent), F32)
+        mixed = jnp.concatenate([total / total[HEAD : HEAD + 1], rest], axis=0)
+        result[rows, :] = mixed.T.astype(BF16)
+
+    finish(total)
+    sums = total[HEAD : HEAD + 1]
     safe = (jnp.min(sums) > LOW) & (jnp.max(sums) < HIGH)
 
     @pl.when(jnp.logical_not(safe))
     def _():
         def peak(chunk, most):
             span = pl.ds(pl.multiple_of(chunk * TOK, TOK), TOK)
-            return jnp.maximum(most, jnp.max(mm(query, key_t[:, span]), axis=1, keepdims=True))
-
-        most = lax.fori_loop(0, TOKENS // TOK, peak, jnp.full((ROWS, 1), -1e30, F32))
+            return jnp.maximum(most, jnp.max(mm(key[span, :], query_t), axis=0, keepdims=True))
+
+        most = lax.fori_loop(0, TOKENS // TOK, peak, jnp.full((1, extent), -1e30, F32))
 
         def mix(chunk, total):
             span = pl.ds(pl.multiple_of(chunk * TOK, TOK), TOK)
-            weights = jnp.exp2((mm(query, key_t[:, span]) - most) * SCALE).astype(BF16)
-            return total + mm(weights, value[span, :])
-
-        total = lax.fori_loop(0, TOKENS // TOK, mix, jnp.zeros((ROWS, LANES), F32))
-        result[rows, :] = (total / total[:, HEAD : HEAD + 1]).astype(BF16)
-
-
-def attend_kernel(plan, rank, received, target_out, stats_out, key_t, value, packed, result, stats):
+            weights = jnp.exp2((mm(key[span, :], query_t) - most) * SCALE).astype(BF16)
+            return total + mm(value_t[:MIXED, span], weights)
+
+        finish(lax.fori_loop(0, TOKENS // TOK, mix, jnp.zeros((MIXED, extent), F32)))
+
+
+def attend_kernel(plan, rank, received, target_out, stats_out, key, value_t, packed, result):
     packed[...] = jnp.zeros((PACKED, LANES), BF16)
     result[...] = jnp.zeros((PACKED, LANES), BF16)
     for source in range(N_SEQ):
         piece = received[source].astype(F32)
         rest = jnp.zeros((LANES - HEAD, TOK), F32)
-        key_t[:, source * TOK : (source + 1) * TOK] = jnp.concatenate([piece[:HEAD], rest], axis=0).astype(BF16)
-        with_ones = jnp.concatenate([piece[HEAD : 2 * HEAD], rest + 1.0], axis=0)
-        value[source * TOK : (source + 1) * TOK, :] = with_ones.T.astype(BF16)
+        span = slice(source * TOK, (source + 1) * TOK)
+        key[span, :] = jnp.concatenate([piece[:HEAD], rest], axis=0).T.astype(BF16)
+        value_t[:, span] = jnp.concatenate([piece[HEAD : 2 * HEAD], rest + 1.0], axis=0).astype(BF16)
         queries = jnp.concatenate([piece[2 * HEAD :], rest], axis=0).T.astype(BF16)
         packed[pl.ds(pl.multiple_of(plan[source], SLOTS), TOK), :] = queries
 
-    def tile(index, _):
-        attend_tile(index, packed, key_t, value, result)
+    def wide(index, _):
+        attend_tile(index * TILES, TILES * ROWS, key, value_t, packed, result)
         return 0
 
-    lax.fori_loop(0, plan[N_SEQ], tile, 0)
+    def narrow(index, _):
+        attend_tile(index, ROWS, key, value_t, packed, result)
+        return 0
+
+    tiles = plan[N_SEQ]
+    lax.fori_loop(0, tiles // TILES, wide, 0)
+    lax.fori_loop(tiles // TILES * TILES, tiles, narrow, 0)
     place = iota((TOK, BLOCK_ROWS), 0).astype(F32)
+    means, squares = [], []
     for source in range(N_SEQ):
         rows = result[pl.ds(pl.multiple_of(plan[source], SLOTS), TOK), :]
         unpack = one_hot(rank[source : source + 1, :] == place)
@@ -309,10 +316,11 @@
         target_out[source] = target.astype(BF16)
         mean = jnp.mean(target, axis=0, keepdims=True)
         centered = target - mean
-        stats[0, source : source + 1, :] = mean
-        stats[1, source : source + 1, :] = jnp.sum(centered * centered, axis=0, keepdims=True)
+        means.append(mean)
+        squares.append(jnp.sum(centered * centered, axis=0, keepdims=True))
+    stats = jnp.concatenate(means + squares, axis=0).astype(BF16)
     for other in range(TARGET_HEADS):
-        stats_out[other] = stats[...]
+        stats_out[other] = stats
 
 
 def attend(plan, rank, received):
@@ -322,16 +330,15 @@
         attend_kernel,
         out_shape=(
             jax.ShapeDtypeStruct((N_SEQ, HEAD, BLOCK_ROWS), BF16),
-            jax.ShapeDtypeStruct((TARGET_HEADS, 2, N_SEQ, BLOCK_ROWS), F32),
+            jax.ShapeDtypeStruct((TARGET_HEADS, STATS, BLOCK_ROWS), BF16),
         ),
         in_specs=[smem, vmem, vmem],
         out_specs=(vmem, vmem),
         scratch_shapes=[
+            pltpu.VMEM((TOKENS, LANES), BF16),
             pltpu.VMEM((LANES, TOKENS), BF16),
-            pltpu.VMEM((TOKENS, LANES), BF16),
             pltpu.VMEM((PACKED, LANES), BF16),
             pltpu.VMEM((PACKED, LANES), BF16),
-            pltpu.VMEM((2, N_SEQ, BLOCK_ROWS), F32),
         ],
         compiler_params=pltpu.CompilerParams(vmem_limit_bytes=16 * 2**20),
         cost_estimate=pl.CostEstimate(flops=12 * 10**9, bytes_accessed=3 * 10**6, transcendentals=16 * 10**6),
@@ -353,10 +360,11 @@
     window = w_proj[:, pl.ds(pl.multiple_of(start, LANES), WINDOW)]
     select = one_hot(iota((HEAD, WINDOW), 1) == iota((HEAD, WINDOW), 0) + (first - start))
     proj = mm_nt(select, window).astype(BF16)
-    means = stats[:, 0]
+    every = stats[...].astype(F32)
+    means = every[:, :N_SEQ]
     mean = jnp.mean(means, axis=0)
     between = means - mean[None]
-    spread = (jnp.sum(stats[:, 1], axis=0) + HEAD * jnp.sum(between * between, axis=0)) / TARGET_WIDTH
+    spread = (jnp.sum(every[:, N_SEQ:], axis=0) + HEAD * jnp.sum(between * between, axis=0)) / TARGET_WIDTH
     scale = lax.rsqrt(spread + 1e-6)
     keep_all = rank[...] >= 0
     share = 1.0 / jnp.full((1, BLOCK_ROWS), count[0], F32)
@@ -393,7 +401,12 @@
     )(me, count, rank, target, stats, mine, other, w_proj)
 
 
-def gradient_kernel(slope, hidden, grad_out):
+def project_kernel(me, lists, slope, hidden, w_proj, grad_out, pred_out):
+    key_valid = lists[pl.ds(me[0], 1), :] >= 0
+    square = (BLOCK_ROWS, BLOCK_ROWS)
+    diagonal = jnp.where(iota(square, 0) == iota(square, 1), jnp.where(key_valid, 1.0, 0.0), 0.0)
+    row_valid = jnp.sum(diagonal, axis=1, keepdims=True) > 0.5
+    pred_out[...] = jnp.where(row_valid, mm(hidden[me[0]], w_proj[...]), 0.0).astype(BF16)
     gradient = jnp.zeros((HEAD, PRED_WIDTH), F32)
     for source in range(N_SEQ):
         rows = slot_rows(hidden, source)
@@ -402,16 +415,20 @@
     grad_out[...] = jnp.concatenate([gradient, rest], axis=0).T
 
 
-def project_gradient(slope, hidden):
-    vmem = pl.BlockSpec(memory_space=pltpu.VMEM)
-    return pl.pallas_call(
-        gradient_kernel,
-        out_shape=jax.ShapeDtypeStruct((PRED_WIDTH, LANES), F32),
-        in_specs=[vmem] * 2,
-        out_specs=vmem,
+def project(me, lists, slope, hidden, w_proj):
+    smem = pl.BlockSpec(memory_space=pltpu.SMEM)
+    vmem = pl.BlockSpec(memory_space=pltpu.VMEM)
+    return pl.pallas_call(
+        project_kernel,
+        out_shape=(
+            jax.ShapeDtypeStruct((PRED_WIDTH, LANES), F32),
+            jax.ShapeDtypeStruct((BLOCK_ROWS, TARGET_WIDTH), BF16),
+        ),
+        in_specs=[smem] + [vmem] * 4,
+        out_specs=(vmem, vmem),
         compiler_params=pltpu.CompilerParams(vmem_limit_bytes=8 * 2**20),
         cost_estimate=pl.CostEstimate(flops=4 * 10**9, bytes_accessed=4 * 10**6, transcendentals=0),
-    )(slope, hidden)
+    )(me, lists, slope, hidden, w_proj)
 
 
 def exchange(pieces, axis):
@@ -431,31 +448,22 @@
 ):
     me = lax.axis_index("seq").astype(jnp.int32).reshape(1)
     beyond = across(context[0], 2)
-    lists, send = pack(me, block_owner, mask_list[0], t_query[0], t_key[0], t_value[0])
+    send = pack(me, block_owner, mask_list[0], t_query[0], t_key[0], t_value[0])
     send, beyond = lax.optimization_barrier((send, beyond))
     received = exchange(send, "seq")
-    rank, local = ranks(lists)
+    lists, rank, local, plan, count = ranks(block_owner, mask_list[0])
     pair = arrange(me, local, context[0], beyond)
     column = [pair] + [along(pair, step) for step in range(1, 4)]
     pieces = column + [across(part, 1) for part in column]
-    filled = (mask_list[0] >= 0).astype(jnp.int32)
-    per_source = jnp.sum(filled.reshape(N_SEQ, N_SEQ, SLOTS), axis=(0, 2))
-    count = jnp.sum(per_source).astype(F32).reshape(1)
-    padded = (per_source + SLOTS - 1) // SLOTS * SLOTS
-    upper = jnp.arange(N_SEQ)[:, None] < jnp.arange(N_SEQ + 1)[None, :]
-    starts = jnp.sum(jnp.where(upper, padded[:, None], 0), axis=0)
-    last = jnp.arange(N_SEQ + 1) == N_SEQ
-    plan = jnp.where(last, (starts + ROWS - 1) // ROWS, starts).astype(jnp.int32)
     hidden = predict(me, lists, pieces, p_gain.reshape(1, PRED_WIDTH), w_query, w_key, w_value)
     received, hidden = lax.optimization_barrier((received, hidden))
     others = across(hidden, 1)
     target, stats = attend(plan, rank, received)
     stats = exchange(stats, "seq")
-    pred_out = project(me, lists, hidden, w_proj)
     slope, loss, rows = compare(me, count, rank, target, stats, hidden, others, w_proj)
     loss, slope = lax.optimization_barrier((loss, slope))
     loss = loss + across(loss, 2)
-    gradient = project_gradient(slope, rows)
+    gradient, pred_out = project(me, lists, slope, rows, w_proj)
     loss, gradient = lax.optimization_barrier((loss, gradient))
     shares = exchange(gradient.reshape(N_SEQ, PRED_WIDTH // N_SEQ, LANES), "clip")
     for mask in (1, 4, 8):

time: 218 us -> 189 us (0.87); the launches traced: 221 us -> 189 us
  Pallas kernels: 100 us -> 68.3 us
  blocking collectives: 0 us -> 18.6 us
  waiting for transfers between devices: 65 us -> 49.5 us
  local copies, waits for them, and re-layouts: 5.76 us -> 1.7 us
    pallas_call x1, Pallas kernels: 73 us -> 43.1 us  [attend(): pl.pallas_call(attend_kernel, out_shape=(jax.ShapeDtypeStruct((N_SEQ, HEA...]
    all_to_all x0 -> x1, blocking collectives: none -> 18.6 us  [exchange(): return lax.all_to_all(pieces, axis, split_axis=0, concat_axis=0, tiled=True)]
    all_to_all x3 -> x2, waiting for transfers between devices: 14.1 us -> 0.01 us  [exchange(): return lax.all_to_all(pieces, axis, split_axis=0, concat_axis=0, tiled=True)]
    unnamed x22 -> x20, local copies, waits for them, and re-layouts: 5.17 us -> 1.19 us
    pallas_call x3 -> x2, Pallas kernels: 8.71 us -> 7.76 us  [the longest x1 5.9 us: pack(): pl.pallas_call(pack_kernel, out_shape=jax.ShapeDtypeStruct((TARGET_HEADS,...]
    all_to_all x3 -> x2, starting transfers between devices: 29.9 us -> 29.3 us  [exchange(): return lax.all_to_all(pieces, axis, split_axis=0, concat_axis=0, tiled=True)]
  transfers between devices with their start and end apart: 16 -> 15, of which waited for: 9 -> 8; matrix products, arithmetic and copies ran while one was open for 1% -> 0% of each run, Pallas kernels for 44% -> 35%
where the time goes in v1:
time: 189 us
  Pallas kernels  68.3 us (36%)
  waiting for transfers between devices  49.5 us (26%)
  starting transfers between devices  47.1 us (25%)
  blocking collectives  18.6 us (10%)
  between operations  3.27 us (2%)
    pallas_call x1, Pallas kernels, attend(): pl.pallas_call(attend_kernel, out_shape=(jax.ShapeDtypeStruct((N_SEQ, HEA...  43.1 us
    ppermute x3, waiting for transfers between devices, along(): lax.ppermute(values, 'seq', [(i, (i + 4 * step) % N_SEQ) for i in range(N...  36.5 us
    all_to_all x2, starting transfers between devices, exchange(): return lax.all_to_all(pieces, axis, split_axis=0, concat_axis=0, tiled=True)  29.3 us
    all_to_all x1, blocking collectives, exchange(): return lax.all_to_all(pieces, axis, split_axis=0, concat_axis=0, tiled=True)  18.6 us
    ppermute x10, waiting for transfers between devices, across(): return lax.ppermute(values, 'seq', [(i, i ^ mask) for i in range(N_SEQ)])  13 us
    pallas_call x1, Pallas kernels, predict(): pl.pallas_call(predict_kernel, out_shape=jax.ShapeDtypeStruct((N_SEQ // 2...  12.9 us
    ppermute x10, starting transfers between devices, across(): return lax.ppermute(values, 'seq', [(i, i ^ mask) for i in range(N_SEQ)])  11.6 us
    ppermute x3, starting transfers between devices, along(): lax.ppermute(values, 'seq', [(i, (i + 4 * step) % N_SEQ) for i in range(N...  6.14 us
  transfers between devices with their start and end apart: 15, of which 8 were waited for; matrix products, arithmetic and copies ran while one was open for 0% of the time, Pallas kernels for 35%

profile of v1, /device:TPU:2, one launch (start us, length us, event | category | flops | bytes accessed | tf_op | source)
XLA Modules:
  0.0 189.1 jit_solution(16651018832604805603)
XLA Ops:
  0.6 7.3 %collective-permute-start = (bf16[256,384]{1,0:T(8,128)(2,1)}, bf16[256,384]{1,0:T(8,128)(2,1)S(1)}, u32[]{:S(2)}, u32[]{:S(2)}) collective-permute-start(bf16[256,384]{1,0:T(8,128)(2,1)} %bitcast.10), channel_id=1, source_target_pairs={{0,2},{1,3},{2,0},{3,1},{4,6},{5,7},{6,4},{7,5},{8,10},{9,11},{10,... | collective-permute-start | bytes 589832 | tf_op jit(solution)/shard_map/ppermute | solution.py:439
  7.9 5.9 %shard_map.131 = bf16[16,264,256]{2,1,0:T(8,128)(2,1)} custom-call(s32[1]{0:T(128)} %bitcast.me, s32[1,16]{1,0:T(1,128)} %owner.3, s32[16,256]{1,0:T(8,128)} %bitcast.12, bf16[256,1408]{1,0:T(8,128)(2,1)} %bitcast.15, bf16[256,1408]{1,0:T(8,128)(2,1)} %bitcast.16, bf16[256,1408]{1,0:T(8,128)(2,1)} %bitcast.17), custom_call_target="tpu_custom_call" | custom-call | flops 3000000000 | bytes 5000000 | tf_op jit(solution)/shard_map/pallas_call | solution.py:106
  13.8 0.0 copy-start.7
  13.8 0.0 copy-start.8
  13.8 0.0 collective-permute-done.beyond
  13.9 12.3 %all-to-all-start = ((bf16[16,264,256]{2,1,0:T(8,128)(2,1)}), bf16[16,264,256]{2,1,0:T(8,128)(2,1)S(1)}, u32[]{:S(2)}, u32[]{:S(2)}) async-start(bf16[16,264,256]{2,1,0:T(8,128)(2,1)} %shard_map.131), calls=%async_computation | async-start | bytes 4325376 | tf_op jit(solution)/shard_map/all_to_all | solution.py:435
  26.2 0.0 copy-start.3
  26.2 0.0 copy-start.9
  26.3 0.0 copy-start.4
  26.3 0.0 copy-start.5
  26.3 0.0 copy-start.6
  26.3 1.6 shard_map.130
  27.9 0.4 shard_map.132.refs_0_
  28.3 2.0 %collective-permute-start.1 = (bf16[2,256,384]{2,1,0:T(8,128)(2,1)S(1)}, bf16[2,256,384]{2,1,0:T(8,128)(2,1)S(1)}, u32[]{:S(2)}, u32[]{:S(2)}) collective-permute-start(bf16[2,256,384]{2,1,0:T(8,128)(2,1)S(1)} %shard_map.132.refs_0_), channel_id=1, source_target_pairs={{0,4},{1,5},{2,6},{3,7},{4,8},{5,9},{6,10},{7,11},{8,12},{9,13},{1... | collective-permute-start | bytes 1179656 | tf_op jit(solution)/shard_map/ppermute | solution.py:443
  30.3 2.7 %collective-permute-start.2 = (bf16[2,256,384]{2,1,0:T(8,128)(2,1)S(1)}, bf16[2,256,384]{2,1,0:T(8,128)(2,1)S(1)}, u32[]{:S(2)}, u32[]{:S(2)}) collective-permute-start(bf16[2,256,384]{2,1,0:T(8,128)(2,1)S(1)} %shard_map.132.refs_0_), channel_id=1, source_target_pairs={{0,8},{1,9},{2,10},{3,11},{4,12},{5,13},{6,14},{7,15},{8,0},{9,1},... | collective-permute-start | bytes 1179656 | tf_op jit(solution)/shard_map/ppermute | solution.py:443
  33.0 1.5 collective-permute-start.3
  34.4 0.0 collective-permute-start.4
  34.4 27.8 %collective-permute-done.1.refs_1_ = bf16[2,256,384]{2,1,0:T(8,128)(2,1)S(1)} collective-permute-done((bf16[2,256,384]{2,1,0:T(8,128)(2,1)S(1)}, bf16[2,256,384]{2,1,0:T(8,128)(2,1)S(1)}, u32[]{:S(2)}, u32[]{:S(2)}) %collective-permute-start.1) | collective-permute-done | bytes 393248 | tf_op jit(solution)/shard_map/ppermute | solution.py:443
  62.2 0.0 collective-permute-start.5
  62.2 8.7 %collective-permute-done.2.refs_2_ = bf16[2,256,384]{2,1,0:T(8,128)(2,1)S(1)} collective-permute-done((bf16[2,256,384]{2,1,0:T(8,128)(2,1)S(1)}, bf16[2,256,384]{2,1,0:T(8,128)(2,1)S(1)}, u32[]{:S(2)}, u32[]{:S(2)}) %collective-permute-start.2) | collective-permute-done | bytes 393248 | tf_op jit(solution)/shard_map/ppermute | solution.py:443
  71.0 0.0 collective-permute-start.6
  71.0 0.0 collective-permute-done.3.refs_3_
  71.0 0.5 collective-permute-start.7
  71.5 0.0 collective-permute-done.4.refs_4_
  71.5 0.0 collective-permute-done.5.refs_5_
  71.5 1.2 collective-permute-done.6.refs_6_
  72.7 0.6 collective-permute-done.7.refs_7_
  73.3 12.9 %shard_map.133.mine = bf16[8,256,384]{2,1,0:T(8,128)(2,1)S(1)} custom-call(s32[1]{0:T(128)} %bitcast.me, s32[16,256]{1,0:T(8,128)S(1)} %get-tuple-element.23.lists, bf16[2,256,384]{2,1,0:T(8,128)(2,1)S(1)} %shard_map.132.refs_0_, bf16[2,256,384]{2,1,0:T(8,128)(2,1)S(1)} %collective-permute-done.1.refs_1_, ...), custom_call_target="tpu_custom_call" | custom-call | flops 12999999488 | bytes 8000000 | tf_op jit(solution)/shard_map/pallas_call | solution.py:233
  86.1 1.1 copy-done
  87.3 0.0 all-to-all-done.received
  87.3 0.1 collective-permute-start.8
  87.4 43.1 %shard_map.134 = (bf16[16,88,256]{2,1,0:T(8,128)(2,1)S(1)}, bf16[16,32,256]{2,1,0:T(8,128)(2,1)S(1)}) custom-call(s32[17]{0:T(128)S(1)} %get-tuple-element.26.plan, f32[16,256]{1,0:T(8,128)S(1)} %get-tuple-element.25.rank, bf16[16,264,256]{2,1,0:T(8,128)(2,1)S(1)} %all-to-all-done.received), custom_call_target="tpu_custom_call" | custom-call | flops 12000000000 | bytes 3000000 | tf_op jit(solution)/shard_map/pallas_call | solution.py:329
  130.5 18.6 %all_to_all.15.stats = bf16[16,32,256]{2,1,0:T(8,128)(2,1)S(1)} all-to-all(bf16[16,32,256]{2,1,0:T(8,128)(2,1)S(1)} %get-tuple-element.32), channel_id=1, replica_groups=mesh['clip'=16,'seq'=16] {'seq'}, dimensions={0} | all-to-all | bytes 524288 | tf_op jit(solution)/shard_map/all_to_all | solution.py:435
  149.1 0.0 collective-permute-done.8.other
  149.1 2.6 %shard_map.135 = (bf16[16,88,256]{2,1,0:T(8,128)(2,1)S(1)}, f32[8,128]{1,0:T(8,128)S(1)}, bf16[16,256,384]{2,1,0:T(8,128)(2,1)S(1)}) custom-call(s32[1]{0:T(128)} %bitcast.me, f32[1]{0:T(128)} %get-tuple-element.24.count, f32[16,256]{1,0:T(8,128)S(1)} %get-tuple-element.25.rank, bf16[16,88,256]{2,1,0:T(8,128)(2,1)S(1)} %get-tuple-element.31.target, ...), custom_call_target="tpu_custom_call" | custom-call | flops 1000000000 | bytes 5000000 | tf_op jit(solution)/shard_map/pallas_call | solution.py:390
  151.7 2.8 %collective-permute-start.9 = (f32[8,128]{1,0:T(8,128)S(1)}, f32[8,128]{1,0:T(8,128)S(1)}, u32[]{:S(2)}, u32[]{:S(2)}) collective-permute-start(f32[8,128]{1,0:T(8,128)S(1)} %get-tuple-element.39), channel_id=1, source_target_pairs={{0,2},{1,3},{2,0},{3,1},{4,6},{5,7},{6,4},{7,5},{8,10},{9,11},{10,... | collective-permute-start | bytes 12296 | tf_op jit(solution)/shard_map/ppermute | solution.py:439
  154.6 1.9 shard_map.136
  156.4 2.9 %collective-permute-done.9 = f32[8,128]{1,0:T(8,128)S(1)} collective-permute-done((f32[8,128]{1,0:T(8,128)S(1)}, f32[8,128]{1,0:T(8,128)S(1)}, u32[]{:S(2)}, u32[]{:S(2)}) %collective-permute-start.9) | collective-permute-done | bytes 4128 | tf_op jit(solution)/shard_map/ppermute | solution.py:439
  159.3 17.0 %all-to-all-start.2 = ((f32[16,24,128]{2,1,0:T(8,128)}), f32[16,24,128]{2,1,0:T(8,128)S(1)}, u32[]{:S(2)}, u32[]{:S(2)}) async-start(f32[16,24,128]{2,1,0:T(8,128)} %bitcast.8), calls=%async_computation.2 | async-start | bytes 393216 | tf_op jit(solution)/shard_map/all_to_all | solution.py:435
  176.3 0.0 collective-permute-start.10
  176.3 1.2 collective-permute-done.10
  177.4 0.0 collective-permute-start.11
  177.4 3.6 %collective-permute-done.11 = f32[8,128]{1,0:T(8,128)S(1)} collective-permute-done((f32[8,128]{1,0:T(8,128)S(1)}, f32[8,128]{1,0:T(8,128)S(1)}, u32[]{:S(2)}, u32[]{:S(2)}) %collective-permute-start.11) | collective-permute-done | bytes 4128 | tf_op jit(solution)/shard_map/ppermute | solution.py:439
  181.1 0.9 collective-permute-start.12
  182.6 3.6 %collective-permute-done.12 = f32[8,128]{1,0:T(8,128)S(1)} collective-permute-done((f32[8,128]{1,0:T(8,128)S(1)}, f32[8,128]{1,0:T(8,128)S(1)}, u32[]{:S(2)}, u32[]{:S(2)}) %collective-permute-start.12) | collective-permute-done | bytes 4128 | tf_op jit(solution)/shard_map/ppermute | solution.py:439
  186.2 0.5 slice.6
  187.3 0.0 all-to-all-done.2
  187.4 0.6 reduce_sum.9
  (17 shorter events, 0.0 us)
Async XLA Ops:
  0.6 13.2 %collective-permute-start = (bf16[256,384]{1,0:T(8,128)(2,1)}, bf16[256,384]{1,0:T(8,128)(2,1)S(1)}, u32[]{:S(2)}, u32[]{:S(2)}) collective-permute-start(bf16[256,384]{1,0:T(8,128)(2,1)} %bitcast.10), channel_id=1, source_target_pairs={{0,2},{1,3},{2,0},{3,1},{4,6},{5,7},{6,4},{7,5},{8,10},{9,11},{10,... | collective-permute-start | bytes 589832 | tf_op jit(solution)/shard_map/ppermute | solution.py:439
  13.8 12.4 %copy-start.7 = (s32[1,16,256]{2,1,0:T(8,128)S(1)}, s32[1,16,256]{2,1,0:T(8,128)}, u32[]{:S(2)}) copy-start(s32[1,16,256]{2,1,0:T(8,128)} %param.15) | copy-start | bytes 49156
  13.8 12.4 %copy-start.8 = (s32[1,16]{1,0:T(1,128)S(1)}, s32[1,16]{1,0:T(1,128)}, u32[]{:S(2)}) copy-start(s32[1,16]{1,0:T(1,128)} %owner.3) | copy-start | bytes 196
  13.9 73.4 %all-to-all-start = ((bf16[16,264,256]{2,1,0:T(8,128)(2,1)}), bf16[16,264,256]{2,1,0:T(8,128)(2,1)S(1)}, u32[]{:S(2)}, u32[]{:S(2)}) async-start(bf16[16,264,256]{2,1,0:T(8,128)(2,1)} %shard_map.131), calls=%async_computation | async-start | bytes 4325376 | tf_op jit(solution)/shard_map/all_to_all | solution.py:435
  26.2 1.7 copy-start.3
  26.2 45.2 %copy-start.9 = (f32[384]{0:T(512)S(1)}, f32[384]{0:T(512)}, u32[]{:S(2)}) copy-start(f32[384]{0:T(512)} %param.17) | copy-start | bytes 4612
  26.3 47.0 %copy-start.4 = (bf16[384,384]{1,0:T(8,128)(2,1)S(1)}, bf16[384,384]{1,0:T(8,128)(2,1)}, u32[]{:S(2)}) copy-start(bf16[384,384]{1,0:T(8,128)(2,1)} %refs_9_.1) | copy-start | bytes 884740
  26.3 47.0 %copy-start.5 = (bf16[384,384]{1,0:T(8,128)(2,1)S(1)}, bf16[384,384]{1,0:T(8,128)(2,1)}, u32[]{:S(2)}) copy-start(bf16[384,384]{1,0:T(8,128)(2,1)} %refs_10_.1) | copy-start | bytes 884740
  26.3 47.0 %copy-start.6 = (bf16[384,384]{1,0:T(8,128)(2,1)S(1)}, bf16[384,384]{1,0:T(8,128)(2,1)}, u32[]{:S(2)}) copy-start(bf16[384,384]{1,0:T(8,128)(2,1)} %refs_11_.1) | copy-start | bytes 884740
  28.3 33.9 %collective-permute-start.1 = (bf16[2,256,384]{2,1,0:T(8,128)(2,1)S(1)}, bf16[2,256,384]{2,1,0:T(8,128)(2,1)S(1)}, u32[]{:S(2)}, u32[]{:S(2)}) collective-permute-start(bf16[2,256,384]{2,1,0:T(8,128)(2,1)S(1)} %shard_map.132.refs_0_), channel_id=1, source_target_pairs={{0,4},{1,5},{2,6},{3,7},{4,8},{5,9},{6,10},{7,11},{8,12},{9,13},{1... | collective-permute-start | bytes 1179656 | tf_op jit(solution)/shard_map/ppermute | solution.py:443
  30.3 40.7 %collective-permute-start.2 = (bf16[2,256,384]{2,1,0:T(8,128)(2,1)S(1)}, bf16[2,256,384]{2,1,0:T(8,128)(2,1)S(1)}, u32[]{:S(2)}, u32[]{:S(2)}) collective-permute-start(bf16[2,256,384]{2,1,0:T(8,128)(2,1)S(1)} %shard_map.132.refs_0_), channel_id=1, source_target_pairs={{0,8},{1,9},{2,10},{3,11},{4,12},{5,13},{6,14},{7,15},{8,0},{9,1},... | collective-permute-start | bytes 1179656 | tf_op jit(solution)/shard_map/ppermute | solution.py:443
  33.0 38.0 %collective-permute-start.3 = (bf16[2,256,384]{2,1,0:T(8,128)(2,1)S(1)}, bf16[2,256,384]{2,1,0:T(8,128)(2,1)S(1)}, u32[]{:S(2)}, u32[]{:S(2)}) collective-permute-start(bf16[2,256,384]{2,1,0:T(8,128)(2,1)S(1)} %shard_map.132.refs_0_), channel_id=1, source_target_pairs={{0,12},{1,13},{2,14},{3,15},{4,0},{5,1},{6,2},{7,3},{8,4},{9,5},{1... | collective-permute-start | bytes 1179656 | tf_op jit(solution)/shard_map/ppermute | solution.py:443
  34.4 37.0 %collective-permute-start.4 = (bf16[2,256,384]{2,1,0:T(8,128)(2,1)S(1)}, bf16[2,256,384]{2,1,0:T(8,128)(2,1)S(1)}, u32[]{:S(2)}, u32[]{:S(2)}) collective-permute-start(bf16[2,256,384]{2,1,0:T(8,128)(2,1)S(1)} %shard_map.132.refs_0_), channel_id=1, source_target_pairs={{0,1},{1,0},{2,3},{3,2},{4,5},{5,4},{6,7},{7,6},{8,9},{9,8},{10,11... | collective-permute-start | bytes 1179656 | tf_op jit(solution)/shard_map/ppermute | solution.py:439
  62.2 9.3 %collective-permute-start.5 = (bf16[2,256,384]{2,1,0:T(8,128)(2,1)S(1)}, bf16[2,256,384]{2,1,0:T(8,128)(2,1)S(1)}, u32[]{:S(2)}, u32[]{:S(2)}) collective-permute-start(bf16[2,256,384]{2,1,0:T(8,128)(2,1)S(1)} %collective-permute-done.1.refs_1_), channel_id=1, source_target_pairs={{0,1},{1,0},{2,3},{3,2},{4,5},{5,4},{6,7},{7,6},{8,9},{9,8},{10,11... | collective-permute-start | bytes 1179656 | tf_op jit(solution)/shard_map/ppermute | solution.py:439
  71.0 1.7 collective-permute-start.6
  71.0 2.3 %collective-permute-start.7 = (bf16[2,256,384]{2,1,0:T(8,128)(2,1)S(1)}, bf16[2,256,384]{2,1,0:T(8,128)(2,1)S(1)}, u32[]{:S(2)}, u32[]{:S(2)}) collective-permute-start(bf16[2,256,384]{2,1,0:T(8,128)(2,1)S(1)} %collective-permute-done.3.refs_3_), channel_id=1, source_target_pairs={{0,1},{1,0},{2,3},{3,2},{4,5},{5,4},{6,7},{7,6},{8,9},{9,8},{10,11... | collective-permute-start | bytes 1179656 | tf_op jit(solution)/shard_map/ppermute | solution.py:439
  86.1 1.1 copy-start
  87.3 61.8 %collective-permute-start.8 = (bf16[8,256,384]{2,1,0:T(8,128)(2,1)}, bf16[8,256,384]{2,1,0:T(8,128)(2,1)S(1)}, u32[]{:S(2)}, u32[]{:S(2)}) collective-permute-start(bf16[8,256,384]{2,1,0:T(8,128)(2,1)} %copy-done), channel_id=1, source_target_pairs={{0,1},{1,0},{2,3},{3,2},{4,5},{5,4},{6,7},{7,6},{8,9},{9,8},{10,11... | collective-permute-start | bytes 4718600 | tf_op jit(solution)/shard_map/ppermute | solution.py:439
  87.4 61.7 %copy-start.1 = (bf16[8,256,384]{2,1,0:T(8,128)(2,1)S(1)}, bf16[8,256,384]{2,1,0:T(8,128)(2,1)}, u32[]{:S(2)}) copy-start(bf16[8,256,384]{2,1,0:T(8,128)(2,1)} %copy-done) | copy-start | bytes 4718596
  87.4 61.7 %copy-start.2 = (bf16[384,1408]{1,0:T(8,128)(2,1)S(1)}, bf16[384,1408]{1,0:T(8,128)(2,1)}, u32[]{:S(2)}) copy-start(bf16[384,1408]{1,0:T(8,128)(2,1)} %w_proj.3) | copy-start | bytes 3244036
  151.7 7.6 %collective-permute-start.9 = (f32[8,128]{1,0:T(8,128)S(1)}, f32[8,128]{1,0:T(8,128)S(1)}, u32[]{:S(2)}, u32[]{:S(2)}) collective-permute-start(f32[8,128]{1,0:T(8,128)S(1)} %get-tuple-element.39), channel_id=1, source_target_pairs={{0,2},{1,3},{2,0},{3,1},{4,6},{5,7},{6,4},{7,5},{8,10},{9,11},{10,... | collective-permute-start | bytes 12296 | tf_op jit(solution)/shard_map/ppermute | solution.py:439
  159.3 28.0 %all-to-all-start.2 = ((f32[16,24,128]{2,1,0:T(8,128)}), f32[16,24,128]{2,1,0:T(8,128)S(1)}, u32[]{:S(2)}, u32[]{:S(2)}) async-start(f32[16,24,128]{2,1,0:T(8,128)} %bitcast.8), calls=%async_computation.2 | async-start | bytes 393216 | tf_op jit(solution)/shard_map/all_to_all | solution.py:435
  176.3 1.2 collective-permute-start.10
  177.4 3.6 %collective-permute-start.11 = (f32[8,128]{1,0:T(8,128)S(1)}, f32[8,128]{1,0:T(8,128)S(1)}, u32[]{:S(2)}, u32[]{:S(2)}) collective-permute-start(f32[8,128]{1,0:T(8,128)S(1)} %add.13), channel_id=1, source_target_pairs={{0,4},{1,5},{2,6},{3,7},{4,0},{5,1},{6,2},{7,3},{8,12},{9,13},{10,... | collective-permute-start | bytes 12296 | tf_op jit(solution)/shard_map/ppermute | solution.py:439
  181.1 5.1 %collective-permute-start.12 = (f32[8,128]{1,0:T(8,128)S(1)}, f32[8,128]{1,0:T(8,128)S(1)}, u32[]{:S(2)}, u32[]{:S(2)}) collective-permute-start(f32[8,128]{1,0:T(8,128)S(1)} %add.14), channel_id=1, source_target_pairs={{0,8},{1,9},{2,10},{3,11},{4,12},{5,13},{6,14},{7,15},{8,0},{9,1},... | collective-permute-start | bytes 12296 | tf_op jit(solution)/shard_map/ppermute | solution.py:439
